TPU v7x, 512 devices: a whole 4x8x8 slice. The times are simulated.
512 devices in a mesh: fsdp: 32 (over y, x), blk: 16 (over z, core).
Axes of the slice: x: 4, y: 8, z: 8, core: 2. Of those that a mesh axis runs over, the one named last changes fastest.
Arguments:
- out_grad: bfloat16 [6144, 8192], P('fsdp'), may hold values from -6 to 6
- layer_input: bfloat16 [6144, 8192], P('fsdp', 'blk'), may hold values from -6 to 6
- gate_pre: bfloat16 [6144, 14336], P('fsdp', 'blk'), may hold values from -8 to 8
- up_pre: bfloat16 [6144, 14336], P('fsdp', 'blk'), may hold values from -6 to 6
- down_weight: bfloat16 [14336, 8192], P('blk', 'fsdp'), may hold values from -0.0625 to 0.0625
- proj_hidden: bfloat16 [14336, 64], P('blk'), may hold values from -0.046875 to 0.046875
- proj_model: bfloat16 [8192, 128], P('blk'), may hold values from -0.0625 to 0.0625
- example_ids: int32 [32, 192], P('fsdp'), may hold values from 0 to 1, as said below
Outputs:
- down_scores: float32 [64, 8192], P('fsdp', 'blk')
- up_scores: float32 [64, 8192], P('fsdp', 'blk')
Inputs may be any that keep to these rules, and one draw needn't show every extreme that they name: `example_ids`: within each row the example number never falls, and each of the 2 examples holds 48 to 144 neighbouring tokens; in some row one example holds exactly 144.
All inputs are finite; a program needn't handle non-finite values.
Results may differ from a plain program's by a relative error of at most 0.0029.
Values may be sent and summed in bfloat16 or wider, within the bound.
No kernel may reach another device: no remote copies, remote signals or barrier semaphores. Data moves between devices by JAX's collectives and lax.ppermute only.
A program may use at most 64 MiB of HBM per device.

v0:
```python
import jax
import jax.numpy as jnp
from jax import lax
from jax.sharding import PartitionSpec as P

EX_DEV = 2


def per_example(left, right, onehot):
    weighted = onehot[:, :, None] * left[:, None, :]
    scores = jnp.einsum("tek,tm->ekm", weighted, right, precision=lax.Precision.HIGHEST)
    return scores.reshape(onehot.shape[1], left.shape[1] * right.shape[1])


def on_device(
    out_grad, layer_input, gate_pre, up_pre, down_weight, proj_hidden, proj_model, example_ids
):
    blk_index = lax.axis_index("blk")
    feat_width = layer_input.shape[1]
    grad_cols = lax.dynamic_slice_in_dim(out_grad, blk_index * feat_width, feat_width, 1)
    grad_part = jnp.dot(grad_cols, proj_model, preferred_element_type=jnp.float32)
    input_part = jnp.dot(layer_input, proj_model, preferred_element_type=jnp.float32)
    grad_side, input_side = lax.psum((grad_part, input_part), "blk")
    silu_gate = jax.nn.silu(gate_pre.astype(jnp.float32))
    hidden = (silu_gate * up_pre.astype(jnp.float32)).astype(jnp.bfloat16)
    hid_part = jnp.dot(hidden, proj_hidden, preferred_element_type=jnp.float32)
    grad_hidden = lax.dot_general(
        out_grad,
        lax.all_gather(down_weight, "fsdp", axis=1, tiled=True),
        (((1,), (1,)), ((), ())),
        preferred_element_type=jnp.float32,
    )
    grad_up = (grad_hidden * silu_gate).astype(jnp.bfloat16)
    up_part = jnp.dot(grad_up, proj_hidden, preferred_element_type=jnp.float32)
    onehot = (example_ids[0][:, None] == jnp.arange(EX_DEV, dtype=jnp.int32)[None, :]).astype(
        jnp.float32
    )
    down_full = per_example(hid_part, grad_side, onehot)
    up_full = per_example(up_part, input_side, onehot)
    down_scores, up_scores = (
        lax.psum_scatter(down_full, "blk", scatter_dimension=1, tiled=True),
        lax.psum_scatter(up_full, "blk", scatter_dimension=1, tiled=True),
    )
    return (down_scores, up_scores)


def solution(mesh):
    in_specs = (
        P("fsdp", None),
        P("fsdp", "blk"),
        P("fsdp", "blk"),
        P("fsdp", "blk"),
        P("blk", "fsdp"),
        P("blk", None),
        P("blk", None),
        P("fsdp", None),
    )
    out_specs = (P("fsdp", "blk"), P("fsdp", "blk"))
    return jax.shard_map(
        on_device, mesh=mesh, in_specs=in_specs, out_specs=out_specs, check_vma=False
    )
```

profile of v0, /device:TPU:2, one launch (start us, length us, event | category | flops | bytes accessed | tf_op | source)
XLA Modules:
  0.0 275.8 jit_solution(12563792531889700550)
XLA Ops:
  8.0 0.0 copy-start
  8.0 0.0 all-reduce.3.cloned.1.call-start
  8.1 2.0 fusion.21
  10.1 0.0 copy-done
  10.1 1.7 fusion.6
  11.8 0.0 all-reduce.3.cloned.1.call-update
  11.8 0.0 all-gather.2.cloned.1.call-start
  11.9 0.5 all-gather.2.cloned.1.call-update
  12.4 0.0 reduce-scatter.7.cloned.1.call-start
  12.5 0.7 compare_convert_fusion
  13.1 1.5 fusion.5
  14.6 114.8 %all-reduce.3.cloned.1.call-done = (f32[192,128]{1,0:T(8,128)}, f32[192,128]{1,0:T(8,128)}) async-done(((f32[192,128]{1,0:T(8,128)}, f32[192,128]{1,0:T(8,128)}), (f32[192,128]{1,0:T(8,128)}, f32[192,128]{1,0:T(8,128)})) %all-reduce.3.cloned.1.call-update) | async-done | bytes 196624 | tf_op jit(solution)/shard_map/psum | solution.py:23
  129.4 1.2 fusion.10
  130.6 0.0 copy-start.2
  130.6 2.7 copy.14
  133.3 0.0 reduce-scatter.7.cloned.1.call-update
  133.3 0.0 copy-start.1
  133.3 0.0 reduce-scatter.9.cloned.1.call-start
  133.4 28.9 %all-gather.2.cloned.1.call-done = bf16[896,8192]{1,0:T(8,128)(2,1)} async-done(((bf16[896,256]{1,0:T(8,128)(2,1)}), bf16[896,8192]{1,0:T(8,128)(2,1)}) %all-gather.2.cloned.1.call-update) | async-done | bytes 14680080 | tf_op jit(solution)/shard_map/all_gather | solution.py:29
  162.3 0.0 copy-done.2
  162.3 10.5 %fusion.1 = f32[192,64]{0,1:T(8,128)S(1)} fusion(bf16[896,64]{0,1:T(8,128)(2,1)S(1)} %copy-done.2, bf16[192,8192]{1,0:T(8,128)(2,1)S(1)} %copy-done, bf16[896,8192]{1,0:T(8,128)(2,1)} %all-gather.2.cloned.1.call-done, bf16[192,896]{1,0:T(8,128)(2,1)} %param.10), kind=kOutput, calls=%fused_computation.2 | convolution fusion | flops 2841796608 | bytes 18333696 | tf_op jit(solution)/shard_map/dot_general | solution.py:34
  172.8 0.0 copy-done.1
  172.8 0.3 fusion.8
  173.1 2.7 copy.15
  175.8 0.0 reduce-scatter.9.cloned.1.call-update
  175.8 24.2 %reduce-scatter.7.cloned.1.call-done = f32[512,2]{1,0:T(8,128)} async-done(((f32[8192,2]{1,0:T(8,128)}), f32[512,2]{1,0:T(8,128)}) %reduce-scatter.7.cloned.1.call-update) | async-done | bytes 4112
  200.0 1.7 copy.11
  201.6 65.3 %reduce-scatter.9.cloned.1.call-done = f32[512,2]{1,0:T(8,128)} async-done(((f32[8192,2]{1,0:T(8,128)}), f32[512,2]{1,0:T(8,128)}) %reduce-scatter.9.cloned.1.call-update) | async-done | bytes 4112
  267.0 1.7 copy.13
Async XLA Ops:
  8.0 2.1 copy-start
  8.0 121.4 %all-reduce.3.cloned.1.call-start = ((), (), s32[]{:S(2)}) async-start(), calls=%async_computation.5 | async-start | bytes 393216 | tf_op jit(solution)/shard_map/psum | solution.py:23
  11.8 150.5 %all-gather.2.cloned.1.call-start = ((), (), s32[]{:S(2)}) async-start(), calls=%async_computation.2 | async-start | bytes 15138816 | tf_op jit(solution)/shard_map/all_gather | solution.py:29
  12.4 187.6 %reduce-scatter.7.cloned.1.call-start = ((), (), s32[]{:S(2)}) async-start(), calls=%async_computation.3 | async-start | bytes 4456448
  130.6 31.7 %copy-start.2 = (bf16[896,64]{0,1:T(8,128)(2,1)S(1)}, bf16[896,64]{0,1:T(8,128)(2,1)}, u32[]{:S(2)}) copy-start(bf16[896,64]{0,1:T(8,128)(2,1)} %param.13) | copy-start | bytes 344068
  133.3 39.5 %copy-start.1 = (f32[192,128]{1,0:T(8,128)S(1)}, f32[192,128]{1,0:T(8,128)}, u32[]{:S(2)}) copy-start(f32[192,128]{1,0:T(8,128)} %get-tuple-element.3) | copy-start | bytes 294916
  133.3 133.7 %reduce-scatter.9.cloned.1.call-start = ((), (), s32[]{:S(2)}) async-start(), calls=%async_computation.4 | async-start | bytes 4456448
Sparse Core Ops, SparseCore 0:
  12.0 117.4 all-reduce.2
  133.4 66.5 reduce-scatter.6
  203.1 63.8 reduce-scatter.8
Sparse Core Ops, SparseCore 1:
  15.8 146.4 all-gather.1
where the time goes:
time: 276 us
  waiting for transfers between devices  234 us (85%)
  matrix products  17.2 us (6%)
  between operations  15.3 us (6%)
  local copies, waits for them, and re-layouts  8.68 us (3%)
    psum x1, waiting for transfers between devices, on_device(): grad_side, input_side = lax.psum((grad_part, input_part), 'blk')  115 us
    unnamed x6, waiting for transfers between devices  90.1 us
    all_gather x1, waiting for transfers between devices, on_device(): lax.all_gather(down_weight, 'fsdp', axis=1, tiled=True)  28.9 us
    dot_general x1, matrix products, on_device(): up_part = jnp.dot(grad_up, proj_hidden, preferred_element_type=jnp.float32)  10.5 us
    unnamed x10, local copies, waits for them, and re-layouts  8.68 us
  transfers between devices with their start and end apart: 4, of which 4 were waited for; matrix products, arithmetic and copies ran while one was open for 8% of the time, Pallas kernels for 0%

commit v1 on v0

--- a/solution.py
+++ b/solution.py
@@ -4,6 +4,11 @@
 from jax.sharding import PartitionSpec as P
 
 EX_DEV = 2
+
+
+def exchange_gather(value, axis, dim):
+    stack = jnp.stack([value] * lax.axis_size(axis))
+    return jnp.concatenate(lax.all_to_all(stack, axis, 0, 0), axis=dim)
 
 
 def per_example(left, right, onehot):
@@ -26,7 +31,7 @@
     hid_part = jnp.dot(hidden, proj_hidden, preferred_element_type=jnp.float32)
     grad_hidden = lax.dot_general(
         out_grad,
-        lax.all_gather(down_weight, "fsdp", axis=1, tiled=True),
+        exchange_gather(down_weight, "fsdp", 1),
         (((1,), (1,)), ((), ())),
         preferred_element_type=jnp.float32,
     )

time: 276 us -> 476 us (1.72)
  the two profiles are of different devices: /device:TPU:2 before, /device:TPU:12 now
where the time goes in v1:
time: 476 us; the launch traced here: 475 us
  waiting for transfers between devices  418 us (88%)
  local copies, waits for them, and re-layouts  19.1 us (4%)
  between operations  13.9 us (3%)
  matrix products  13.4 us (3%)
  starting transfers between devices  10.8 us (2%)
    all_to_all x1, waiting for transfers between devices, exchange_gather(): return jnp.concatenate(lax.all_to_all(stack, axis, 0, 0), axis=dim)  204 us
    psum x1, waiting for transfers between devices, on_device(): grad_side, input_side = lax.psum((grad_part, input_part), 'blk')  118 us
    unnamed x5, waiting for transfers between devices  96.6 us
    unnamed x17, local copies, waits for them, and re-layouts  10.7 us
    all_to_all x1, starting transfers between devices, exchange_gather(): return jnp.concatenate(lax.all_to_all(stack, axis, 0, 0), axis=dim)  10.6 us
  transfers between devices with their start and end apart: 4, of which 3 were waited for; matrix products, arithmetic and copies ran while one was open for 4% of the time, Pallas kernels for 0%

profile of v1, /device:TPU:12, one launch (start us, length us, event | category | flops | bytes accessed | tf_op | source)
XLA Modules:
  0.0 475.4 jit_solution(6478904892759960711)
XLA Ops:
  7.2 0.0 copy-start
  7.2 2.2 copy.11
  9.3 8.3 %stack.2 = bf16[32,896,256]{1,2,0:T(8,128)(2,1)} broadcast(bf16[896,256]{0,1:T(8,128)(2,1)} %copy.11), dimensions={1,2} | broadcast | bytes 15138816 | tf_op jit(solution)/shard_map/stack | solution.py:10
  17.6 10.6 %all-to-all-start = ((bf16[32,896,256]{1,2,0:T(8,128)(2,1)}), bf16[32,896,256]{1,2,0:T(8,128)(2,1)}, u32[]{:S(2)}, u32[]{:S(2)}) async-start(bf16[32,896,256]{1,2,0:T(8,128)(2,1)} %stack.2), calls=%async_computation | async-start | bytes 29360128 | tf_op jit(solution)/shard_map/all_to_all | solution.py:11
  28.3 0.0 copy-start.4
  28.3 0.0 all-reduce.3.cloned.1.call-start
  28.4 0.0 copy-done
  28.4 0.0 copy-done.1
  28.4 0.8 fusion.6
  29.2 0.0 copy-done.2
  29.2 0.8 fusion.21
  30.1 0.0 all-reduce.3.cloned.1.call-update
  30.1 0.0 reduce-scatter.7.cloned.1.call-start
  30.1 1.5 fusion.5
  31.6 0.0 copy-done.4
  31.6 117.6 %all-reduce.3.cloned.1.call-done = (f32[192,128]{1,0:T(8,128)}, f32[192,128]{1,0:T(8,128)}) async-done(((f32[192,128]{1,0:T(8,128)}, f32[192,128]{1,0:T(8,128)}), (f32[192,128]{1,0:T(8,128)}, f32[192,128]{1,0:T(8,128)})) %all-reduce.3.cloned.1.call-update) | async-done | bytes 196624 | tf_op jit(solution)/shard_map/psum | solution.py:28
  149.2 1.2 fusion.10
  150.4 0.0 copy-start.5
  150.4 2.6 copy.16
  153.0 0.0 reduce-scatter.7.cloned.1.call-update
  153.0 0.0 reduce-scatter.9.cloned.1.call-start
  153.1 204.2 %all-to-all-done = bf16[32,896,256]{1,2,0:T(8,128)(2,1)} async-done(((bf16[32,896,256]{1,2,0:T(8,128)(2,1)}), bf16[32,896,256]{1,2,0:T(8,128)(2,1)}, u32[]{:S(2)}, u32[]{:S(2)}) %all-to-all-start) | async-done | bytes 14680096 | tf_op jit(solution)/shard_map/all_to_all | solution.py:11
  357.3 0.0 copy-done.5
  357.3 8.8 %fusion.1 = f32[192,64]{0,1:T(8,128)S(1)} fusion(bf16[896,64]{0,1:T(8,128)(2,1)S(1)} %copy-done.5, bf16[192,8192]{1,0:T(8,128)(2,1)S(1)} %copy-done, bf16[896,8192]{0,1:T(8,128)(2,1)} %bitcast.3, bf16[192,896]{1,0:T(8,128)(2,1)} %param.10), kind=kOutput, calls=%fused_computation.2 | convolution fusion | flops 2841796608 | bytes 18333696 | tf_op jit(solution)/shard_map/dot_general | solution.py:39
  366.1 0.0 copy-done.3
  366.1 0.3 fusion.8
  366.4 2.6 copy.17
  369.0 0.0 reduce-scatter.9.cloned.1.call-update
  369.0 0.0 reduce-scatter.7.cloned.1.call-done
  369.1 1.7 copy.13
  370.7 96.5 %reduce-scatter.9.cloned.1.call-done = f32[512,2]{1,0:T(8,128)} async-done(((f32[8192,2]{1,0:T(8,128)}), f32[512,2]{1,0:T(8,128)}) %reduce-scatter.9.cloned.1.call-update) | async-done | bytes 4112
  467.3 1.7 copy.15
  (4 shorter events, 0.0 us)
Async XLA Ops:
  7.2 21.2 %copy-start = (bf16[192,8192]{1,0:T(8,128)(2,1)S(1)}, bf16[192,8192]{1,0:T(8,128)(2,1)}, u32[]{:S(2)}) copy-start(bf16[192,8192]{1,0:T(8,128)(2,1)} %param.8) | copy-start | bytes 9437188
  17.6 10.7 %copy-start.1 = (bf16[512,128]{1,0:T(8,128)(2,1)S(1)}, bf16[512,128]{1,0:T(8,128)(2,1)}, u32[]{:S(2)}) copy-start(bf16[512,128]{1,0:T(8,128)(2,1)} %param.14) | copy-start | bytes 393220
  17.6 11.6 %copy-start.2 = (bf16[192,512]{1,0:T(8,128)(2,1)S(1)}, bf16[192,512]{1,0:T(8,128)(2,1)}, u32[]{:S(2)}) copy-start(bf16[192,512]{1,0:T(8,128)(2,1)} %param.9) | copy-start | bytes 589828
  17.6 339.6 %all-to-all-start = ((bf16[32,896,256]{1,2,0:T(8,128)(2,1)}), bf16[32,896,256]{1,2,0:T(8,128)(2,1)}, u32[]{:S(2)}, u32[]{:S(2)}) async-start(bf16[32,896,256]{1,2,0:T(8,128)(2,1)} %stack.2), calls=%async_computation | async-start | bytes 29360128 | tf_op jit(solution)/shard_map/all_to_all | solution.py:11
  28.3 3.3 copy-start.4
  28.3 120.9 %all-reduce.3.cloned.1.call-start = ((), (), s32[]{:S(2)}) async-start(), calls=%async_computation.5 | async-start | bytes 393216 | tf_op jit(solution)/shard_map/psum | solution.py:28
  30.1 339.0 %reduce-scatter.7.cloned.1.call-start = ((), (), s32[]{:S(2)}) async-start(), calls=%async_computation.3 | async-start | bytes 4456448
  150.4 206.9 %copy-start.5 = (bf16[896,64]{0,1:T(8,128)(2,1)S(1)}, bf16[896,64]{0,1:T(8,128)(2,1)}, u32[]{:S(2)}) copy-start(bf16[896,64]{0,1:T(8,128)(2,1)} %param.13) | copy-start | bytes 344068
  153.0 314.2 %reduce-scatter.9.cloned.1.call-start = ((), (), s32[]{:S(2)}) async-start(), calls=%async_computation.4 | async-start | bytes 4456448
  357.3 8.8 %copy-start.3 = (f32[192,128]{1,0:T(8,128)S(1)}, f32[192,128]{1,0:T(8,128)}, u32[]{:S(2)}) copy-start(f32[192,128]{1,0:T(8,128)} %get-tuple-element.3) | copy-start | bytes 294916
Sparse Core Ops, SparseCore 0:
  31.6 117.6 all-reduce.2
  153.2 68.3 reduce-scatter.6
  369.2 98.0 reduce-scatter.8
